TPU v7x, 256 devices: a whole 4x4x8 slice. The times are simulated.
256 devices in a mesh: dp: 4 (over z_hi), space: 64 (over x, z_lo, y, core).
Axes of the slice: x: 4, y: 4, z: 8 (z_hi: 4, z_lo: 2; z = z_hi * 2 + z_lo), core: 2. Of those that a mesh axis runs over, the one named last changes fastest.
Arguments:
- density_cubes: bfloat16 [4, 4, 512, 64, 128], P('dp', None, 'space'), may hold values from -6 to 6
- first_kernel: bfloat16 [16, 4, 3, 3, 3], replicated, may hold values from -0.625 to 0.625
- second_kernel: bfloat16 [32, 16, 3, 3, 3], replicated, may hold values from -0.3125 to 0.3125
- third_kernel: bfloat16 [64, 32, 3, 3, 3], replicated, may hold values from -0.21875 to 0.21875
- cotangent: bfloat16 [4, 64, 64, 8, 16], P('dp', 'space'), may hold values from -0.03125 to 0.03125
Outputs:
- features: bfloat16 [4, 64, 64, 8, 16], P('dp', 'space')
- first_grad: float32 [16, 4, 3, 3, 3], replicated
- second_grad: float32 [32, 16, 3, 3, 3], replicated
- third_grad: float32 [64, 32, 3, 3, 3], P('space')
All inputs are finite; a program needn't handle non-finite values.
Results may differ from a plain program's by a relative error of at most 0.012.
Values may be sent and summed in bfloat16 or wider, within the bound.
No kernel may reach another device: no remote copies, remote signals or barrier semaphores. Data moves between devices by JAX's collectives and lax.ppermute only.
A program may use at most 320 MiB of HBM per device.

v0:
```python
import jax
import jax.numpy as jnp
from jax import lax
from jax.sharding import PartitionSpec as P


def passed_along(block, axis, distance):
    devices = range(lax.axis_size(axis))
    route = [(i - distance, i) for i in devices if i - distance in devices]
    return lax.ppermute(block, axis, route)


def convolve(inputs, kernel, padding):
    return lax.conv_general_dilated(
        inputs,
        kernel,
        (2, 2, 2),
        padding,
        dimension_numbers=("NCDHW", "OIDHW", "NCDHW"),
        preferred_element_type=jnp.float32,
    )


def input_gradient(deltas, kernel, padding):
    flipped = kernel[:, :, ::-1, ::-1, ::-1]
    return lax.conv_general_dilated(
        deltas,
        flipped,
        (1, 1, 1),
        padding,
        lhs_dilation=(2, 2, 2),
        dimension_numbers=("NCDHW", "IODHW", "NCDHW"),
        preferred_element_type=jnp.float32,
    )


def kernel_gradient(inputs, deltas, padding):
    result = lax.conv_general_dilated(
        inputs,
        deltas,
        (1, 1, 1),
        padding,
        rhs_dilation=(2, 2, 2),
        dimension_numbers=("CNDHW", "IODHW", "NCDHW"),
        preferred_element_type=jnp.float32,
    )
    return jnp.transpose(result, (1, 0, 2, 3, 4))


def activate(preact):
    return jax.nn.gelu(preact, approximate=True)


def gelu_backward(preact, upstream):
    unused, pullback = jax.vjp(activate, preact)
    return pullback(upstream)[0]


def fold_back(widened, returned):
    inner = widened[:, :, 1:]
    return jnp.concatenate([inner[:, :, :-1], inner[:, :, -1:] + returned], axis=2)


def shards(density_cubes, first_kernel, second_kernel, third_kernel, cotangent):
    forward_pads = ((0, 0), (1, 0), (1, 0))
    transpose_pads = ((2, 2), (1, 2), (1, 2))
    lower_plane = passed_along(density_cubes[:, :, -1:], "space", 1)
    widened_cubes = jnp.concatenate([lower_plane, density_cubes], axis=2)
    first_pre = convolve(widened_cubes, first_kernel, forward_pads)
    first_act = activate(first_pre).astype(jnp.bfloat16)
    lower_plane = passed_along(first_act[:, :, -1:], "space", 1)
    widened_first = jnp.concatenate([lower_plane, first_act], axis=2)
    second_pre = convolve(widened_first, second_kernel, forward_pads)
    second_act = activate(second_pre).astype(jnp.bfloat16)
    lower_plane = passed_along(second_act[:, :, -1:], "space", 1)
    widened_second = jnp.concatenate([lower_plane, second_act], axis=2)
    third_pre = convolve(widened_second, third_kernel, forward_pads)
    features = lax.all_to_all(
        activate(third_pre).astype(jnp.bfloat16), "space", split_axis=1, concat_axis=2, tiled=True
    )
    arrived = lax.all_to_all(cotangent, "space", split_axis=2, concat_axis=1, tiled=True)
    delta_third = gelu_backward(third_pre, arrived.astype(jnp.float32)).astype(jnp.bfloat16)
    local_third = kernel_gradient(widened_second, delta_third, forward_pads)
    owned_third = lax.psum_scatter(local_third, "space", scatter_dimension=0, tiled=True)
    third_grad = lax.psum(owned_third, "dp")
    widened_upstream = input_gradient(delta_third, third_kernel, transpose_pads)
    returned = passed_along(widened_upstream[:, :, :1].astype(jnp.bfloat16), "space", -1).astype(
        jnp.float32
    )
    upstream_second = fold_back(widened_upstream, returned)
    delta_second = gelu_backward(second_pre, upstream_second).astype(jnp.bfloat16)
    local_second = kernel_gradient(widened_first, delta_second, forward_pads)
    widened_upstream_first = input_gradient(delta_second, second_kernel, transpose_pads)
    returned_first = passed_along(
        widened_upstream_first[:, :, :1].astype(jnp.bfloat16), "space", -1
    ).astype(jnp.float32)
    upstream_first = fold_back(widened_upstream_first, returned_first)
    delta_first = gelu_backward(first_pre, upstream_first).astype(jnp.bfloat16)
    local_first = kernel_gradient(widened_cubes, delta_first, forward_pads)
    first_grad, second_grad = lax.psum((local_first, local_second), ("dp", "space"))
    return (features, first_grad, second_grad, third_grad)


def solution(mesh):
    in_specs = (
        P("dp", None, "space", None, None),
        P(),
        P(),
        P(),
        P("dp", "space", None, None, None),
    )
    out_specs = (P("dp", "space", None, None, None), P(), P(), P("space", None, None, None, None))
    return jax.shard_map(shards, mesh=mesh, in_specs=in_specs, out_specs=out_specs, check_vma=False)
```

profile of v0, /device:TPU:1, one launch (start us, length us, event | category | flops | bytes accessed | tf_op | source)
XLA Modules:
  0.0 757.2 jit_solution(13227399613651763805)
XLA Ops:
  8.1 4.6 collective-permute-start
  17.4 10.9 %copy.249 = bf16[4,9,64,1,8,18]{4,0,5,2,1,3:T(4,128)(2,1)} copy(bf16[4,9,64,1,8,18]{2,0,5,4,1,3:T(4,128)(2,1)S(1)} %bitcast.204) | data formatting | bytes 1327104 | tf_op jit(solution)/shard_map/conv_general_dilated | solution.py:14
  28.3 2.0 slice.80
  30.3 15.7 %fusion.3 = f32[4,32,8,9,16]{4,2,3,1,0:T(8,128)} fusion(bf16[16,4,3,3,3]{0,1,4,3,2:T(4,128)(2,1)S(1)} %copy-done.17, bf16[4,9,64,1,7,2]{4,0,5,2,1,3:T(4,128)(2,1)S(1)} %slice.80, bf16[4,9,64,1,8,18]{4,0,5,2,1,3:T(4,128)(2,1)} %copy.249), kind=kOutput, calls=%fused_computation.4 | convolution fusion | flops 33730560 | bytes 1321344 | tf_op jit(solution)/shard_map/conv_general_dilated | solution.py:14
  46.0 3.8 copy.250
  49.9 4.2 broadcast_select_fusion.1
  55.4 4.3 collective-permute-start.1
  60.5 11.0 %all-to-all-start.1 = ((bf16[1,1,64,8,16]{4,3,1,0,2:T(8,128)(2,1)}), bf16[1,1,64,8,16]{4,3,1,0,2:T(8,128)(2,1)S(1)}, u32[]{:S(2)}, u32[]{:S(2)}) async-start(bf16[1,1,64,8,16]{4,3,1,0,2:T(8,128)(2,1)} %copy.268), calls=%async_computation.1 | async-start | bytes 262144 | tf_op jit(solution)/shard_map/all_to_all | solution.py:81
  72.9 6.7 copy.303
  80.4 16.7 %pad_maximum_fusion = bf16[1,16,5,32,64]{1,0,4,3,2:T(2,128)(2,1)} fusion(bf16[1,16,4,32,64]{1,0,4,3,2:T(2,128)(2,1)} %bitcast.196, bf16[1,16,1,32,64]{1,0,4,3,2:T(2,128)(2,1)S(1)} %copy.253), kind=kLoop, calls=%fused_computation.8 | loop fusion | flops 163840 | bytes 655360 | tf_op jit(solution)/shard_map/concatenate | solution.py:72
  97.1 11.4 %copy.254 = bf16[1,16,5,32,64]{4,3,2,1,0:T(8,128)(2,1)S(1)} copy(bf16[1,16,5,32,64]{1,0,4,3,2:T(2,128)(2,1)} %pad_maximum_fusion) | data formatting | bytes 655360 | tf_op jit(solution)/shard_map/concatenate | solution.py:72
  109.8 3.7 copy.257
  114.8 5.4 subtract_multiply_fusion.1
  121.2 4.1 collective-permute-start.2
  126.0 40.1 %copy.296 = bf16[1,4,9,64,128]{1,0,4,3,2:T(2,128)(2,1)} copy(bf16[1,4,9,64,128]{4,3,2,1,0:T(8,128)(2,1)S(1)} %copy-done.6) | data formatting | bytes 1179648 | tf_op jit(solution)/shard_map/concatenate | solution.py:68
  168.4 2.2 pad_maximum_fusion.2
  175.2 2.6 fusion.76
  180.2 8.2 %all-to-all-start = ((bf16[1,64,1,8,16]{4,3,2,0,1:T(8,128)(2,1)}), bf16[1,64,1,8,16]{4,3,2,0,1:T(8,128)(2,1)S(1)}, u32[]{:S(2)}, u32[]{:S(2)}) async-start(bf16[1,64,1,8,16]{4,3,2,0,1:T(8,128)(2,1)} %copy.267), calls=%async_computation | async-start | bytes 262144 | tf_op jit(solution)/shard_map/all_to_all | solution.py:78
  190.4 2.5 collective-permute-start.3
  194.6 2.4 all-to-all-done
  200.0 13.7 %fusion.48 = f32[32,16,3,3,3]{0,1,4,3,2:T(8,128)} fusion(bf16[1,16,5,32,64]{1,0,4,3,2:T(2,128)(2,1)} %pad_maximum_fusion, bf16[1,32,2,16,32]{1,3,4,0,2:T(8,128)(2,1)S(1)} %fusion.42), kind=kOutput, calls=%fused_computation.77 | convolution fusion | flops 27432960 | bytes 448512 | tf_op jit(solution)/shard_map/transpose | solution.py:47
  213.9 3.4 broadcast_select_fusion
  217.4 2.6 copy-done.2
  220.0 2.2 slice.106
  223.6 2.3 collective-permute-start.4
  225.9 2.8 copy.291
  233.1 4.4 fusion.17
  237.5 6.8 copy.297
  244.3 87.8 %fusion.95 = f32[16,4,3,3,3]{0,1,4,3,2:T(4,128)S(1)} fusion(bf16[1,4,9,64,128]{1,0,4,3,2:T(2,128)(2,1)} %copy.296, bf16[1,16,4,32,64]{1,0,4,3,2:T(2,128)(2,1)} %copy.297), kind=kOutput, calls=%fused_computation.145 | convolution fusion | flops 27870720 | bytes 858880 | tf_op jit(solution)/shard_map/transpose | solution.py:47
  332.1 88.7 %all-reduce.1 = (f32[16,4,3,3,3]{0,1,4,3,2:T(4,128)}, f32[32,16,3,3,3]{0,1,4,3,2:T(8,128)}) all-reduce(f32[16,4,3,3,3]{0,1,4,3,2:T(4,128)S(1)} %fusion.95, f32[32,16,3,3,3]{0,1,4,3,2:T(8,128)S(1)} %copy-done.10), channel_id=1, replica_groups=mesh['dp'=4,'space'=64] {'dp','space'}, use_global_device_ids=true, to_apply=%region_0.0 | all-reduce | flops 15552 | bytes 124416 | tf_op jit(solution)/shard_map/psum | solution.py:100
  420.8 311.6 %all-reduce.4.cloned.1.call-done = f32[64,32,3,3,3]{1,0,4,3,2:T(8,128)} async-done(((f32[64,32,3,3,3]{1,0,4,3,2:T(8,128)}), f32[64,32,3,3,3]{1,0,4,3,2:T(8,128)}) %all-reduce.4.cloned.1.call-update) | async-done | bytes 221200
  733.9 16.2 %psum.23 = f32[1,32,3,3,3]{1,0,4,3,2:T(1,128)} all-reduce(f32[1,32,3,3,3]{1,0,4,3,2:T(1,128)S(1)} %constant_dynamic-slice_fusion), channel_id=1, replica_groups=mesh['dp'=4,'space'=64] {'dp'}, use_global_device_ids=true, to_apply=%region_3.0 | all-reduce | flops 864 | bytes 6912 | tf_op jit(solution)/shard_map/psum | solution.py:85
  (116 shorter events, 37.4 us)
Async XLA Ops:
  7.2 167.1 %copy-start = (bf16[64,32,3,3,3]{0,1,4,3,2:T(8,128)(2,1)S(1)}, bf16[64,32,3,3,3]{0,1,4,3,2:T(8,128)(2,1)}, u32[]{:S(2)}) copy-start(bf16[64,32,3,3,3]{0,1,4,3,2:T(8,128)(2,1)} %param.8) | copy-start | bytes 331780
  8.1 5.9 collective-permute-start
  15.1 0.8 copy-start.5
  28.3 2.0 copy-start.17
  46.0 3.8 copy-start.16
  49.9 9.8 %copy-start.13 = (bf16[1,1,64,8,16]{2,4,3,1,0:T(8,128)(2,1)S(1)}, bf16[1,1,64,8,16]{2,4,3,1,0:T(8,128)(2,1)}, u32[]{:S(2)}) copy-start(bf16[1,1,64,8,16]{2,4,3,1,0:T(8,128)(2,1)} %param.9) | copy-start | bytes 49156
  54.1 1.0 copy-start.4
  55.4 24.2 %collective-permute-start.1 = (bf16[1,16,1,32,64]{4,3,2,1,0:T(8,128)(2,1)S(1)}, bf16[1,16,1,32,64]{4,3,2,1,0:T(8,128)(2,1)S(1)}, u32[]{:S(2)}, u32[]{:S(2)}) collective-permute-start(bf16[1,16,1,32,64]{4,3,2,1,0:T(8,128)(2,1)S(1)} %copy.251), channel_id=1, source_target_pairs={{0,1},{1,2},{2,3},{3,4},{4,5},{5,6},{6,7},{7,8},{8,9},{9,10},{10,1... | collective-permute-start | bytes 196616 | tf_op jit(solution)/shard_map/ppermute | solution.py:10
  60.5 65.4 %all-to-all-start.1 = ((bf16[1,1,64,8,16]{4,3,1,0,2:T(8,128)(2,1)}), bf16[1,1,64,8,16]{4,3,1,0,2:T(8,128)(2,1)S(1)}, u32[]{:S(2)}, u32[]{:S(2)}) async-start(bf16[1,1,64,8,16]{4,3,1,0,2:T(8,128)(2,1)} %copy.268), calls=%async_computation.1 | async-start | bytes 262144 | tf_op jit(solution)/shard_map/all_to_all | solution.py:81
  109.8 5.0 copy-start.11
  109.8 5.0 copy-start.19
  114.8 10.5 %copy-start.18 = (u32[256]{0:T(256)S(1)}, u32[256]{0:T(256)}, u32[]{:S(2)}) copy-start(u32[256]{0:T(256)} %constant.53) | copy-start | bytes 3076
  114.8 11.2 %copy-start.6 = (bf16[1,4,9,64,128]{4,3,2,1,0:T(8,128)(2,1)S(1)}, bf16[1,4,9,64,128]{4,3,2,1,0:T(8,128)(2,1)}, u32[]{:S(2)}) copy-start(bf16[1,4,9,64,128]{4,3,2,1,0:T(8,128)(2,1)} %copy-done.5) | copy-start | bytes 1769476
  121.2 47.2 %collective-permute-start.2 = (bf16[1,32,1,16,32]{1,0,4,3,2:T(2,128)(2,1)}, bf16[1,32,1,16,32]{1,0,4,3,2:T(2,128)(2,1)}, u32[]{:S(2)}, u32[]{:S(2)}) collective-permute-start(bf16[1,32,1,16,32]{1,0,4,3,2:T(2,128)(2,1)} %bitcast.195), channel_id=1, source_target_pairs={{0,1},{1,2},{2,3},{3,4},{4,5},{5,6},{6,7},{7,8},{8,9},{9,10},{10,1... | collective-permute-start | bytes 98312 | tf_op jit(solution)/shard_map/ppermute | solution.py:10
  166.1 1.1 copy-start.9
  166.1 1.2 copy-start.8
  170.5 3.7 copy-start.20
  175.0 2.9 copy-start.15
  180.2 18.5 %copy-start.7 = (f32[2,16,8,5,32]{4,1,3,2,0:T(8,128)S(1)}, f32[2,16,8,5,32]{4,1,3,2,0:T(8,128)}, u32[]{:S(2)}) copy-start(f32[2,16,8,5,32]{4,1,3,2,0:T(8,128)} %copy.281) | copy-start | bytes 491524
  180.2 16.8 %all-to-all-start = ((bf16[1,64,1,8,16]{4,3,2,0,1:T(8,128)(2,1)}), bf16[1,64,1,8,16]{4,3,2,0,1:T(8,128)(2,1)S(1)}, u32[]{:S(2)}, u32[]{:S(2)}) async-start(bf16[1,64,1,8,16]{4,3,2,0,1:T(8,128)(2,1)} %copy.267), calls=%async_computation | async-start | bytes 262144 | tf_op jit(solution)/shard_map/all_to_all | solution.py:78
  188.5 543.9 %all-reduce.4.cloned.1.call-start = ((), (), s32[]{:S(2)}) async-start(), calls=%async_computation.2 | async-start | bytes 1769472
  190.4 7.3 collective-permute-start.3
  199.9 13.9 %copy-start.12 = (bf16[32,16,3,3,3]{0,1,4,3,2:T(8,128)(2,1)S(1)}, bf16[32,16,3,3,3]{0,1,4,3,2:T(8,128)(2,1)}, u32[]{:S(2)}) copy-start(bf16[32,16,3,3,3]{0,1,4,3,2:T(8,128)(2,1)} %param.7) | copy-start | bytes 82948
  200.0 13.9 %copy-start.14 = (pred[8,10]{0,1:T(8,128)(4,1)S(1)}, pred[8,10]{0,1:T(8,128)(4,1)}, u32[]{:S(2)}) copy-start(pred[8,10]{0,1:T(8,128)(4,1)} %constant.49) | copy-start | bytes 244
  217.3 2.7 copy-start.2
  223.6 8.4 %collective-permute-start.4 = (bf16[1,16,1,32,64]{3,1,4,2,0:T(8,128)(2,1)}, bf16[1,16,1,32,64]{3,1,4,2,0:T(8,128)(2,1)}, u32[]{:S(2)}, u32[]{:S(2)}) collective-permute-start(bf16[1,16,1,32,64]{3,1,4,2,0:T(8,128)(2,1)} %slice_bitcast_fusion.10), channel_id=1, source_target_pairs={{1,0},{2,1},{3,2},{4,3},{5,4},{6,5},{7,6},{8,7},{9,8},{10,9},{11,1... | collective-permute-start | bytes 196616 | tf_op jit(solution)/shard_map/ppermute | solution.py:10
  228.7 1.9 slice-start
  229.9 3.2 copy-start.3
  244.3 87.8 %copy-start.10 = (f32[32,16,3,3,3]{0,1,4,3,2:T(8,128)S(1)}, f32[32,16,3,3,3]{0,1,4,3,2:T(8,128)}, u32[]{:S(2)}) copy-start(f32[32,16,3,3,3]{0,1,4,3,2:T(8,128)} %fusion.48) | copy-start | bytes 165892
  244.3 505.8 %copy-start.1 = (bf16[64,32,3,3,3]{0,1,4,3,2:T(8,128)(2,1)S(1)}, bf16[64,32,3,3,3]{0,1,4,3,2:T(8,128)(2,1)}, u32[]{:S(2)}) copy-start(bf16[64,32,3,3,3]{0,1,4,3,2:T(8,128)(2,1)} %param.8) | copy-start | bytes 331780
Sparse Core Ops, SparseCore 0:
  192.0 540.3 all-reduce.3
where the time goes:
time: 768 us; the launch traced here: 757 us
  waiting for transfers between devices  316 us (41%)
  matrix products  130 us (17%)
  local copies, waits for them, and re-layouts  123 us (16%)
  blocking collectives  105 us (14%)
  starting transfers between devices  37 us (5%)
  other arithmetic  30.8 us (4%)
  between operations  14.9 us (2%)
    unnamed x2, waiting for transfers between devices  312 us
    transpose x3, matrix products, kernel_gradient(): return jnp.transpose(result, (1, 0, 2, 3, 4))  104 us
    psum x1, blocking collectives, shards(): lax.psum((local_first, local_second), ('dp', 'space'))  88.7 us
    concatenate x3, local copies, waits for them, and re-layouts, shards(): widened_cubes = jnp.concatenate([lower_plane, density_cubes], axis=2)  41.8 us
    conv_general_dilated x9, local copies, waits for them, and re-layouts, convolve(): lax.conv_general_dilated(inputs, kernel, (2, 2, 2), padding, dimension_nu...  22.9 us
    conv_general_dilated x3, matrix products, convolve(): lax.conv_general_dilated(inputs, kernel, (2, 2, 2), padding, dimension_nu...  21.8 us
    unnamed x53, local copies, waits for them, and re-layouts  19.9 us
    ppermute x5, starting transfers between devices, passed_along(): return lax.ppermute(block, axis, route)  17.7 us
  transfers between devices with their start and end apart: 8, of which 3 were waited for; matrix products, arithmetic and copies ran while one was open for 30% of the time, Pallas kernels for 0%

commit v1 on v0

v1 whole, which is shorter than its diff:
```python
import math

import jax
import jax.numpy as jnp
import numpy as np
from jax import lax
from jax.experimental import pallas as pl
from jax.experimental.pallas import tpu as pltpu
from jax.sharding import PartitionSpec as P


BF16 = jnp.bfloat16
F32 = jnp.float32
CELLS = 128
ROWS0, ROWS1, ROWS2 = 48, 80, 96
SCALE = math.sqrt(2.0 / math.pi)
SPACE = ("x", "z", "y", "core")
NEAR = ("z", "y", "core")
FAR = ("dp", "x")


def first_selection():
    chosen = np.zeros((4, 4, 32, 9, ROWS0), np.float32)
    for ry in range(4):
        for c in range(4):
            for kx in range(3):
                for ky in range(3):
                    for kz in range(3):
                        y = 2 * ry + ky - 1
                        row = 32 + c if y < 0 else 8 * c + y
                        chosen[ry, c, 9 * kx + 3 * ky + kz, 3 * kx + kz, row] = 1
    return chosen.reshape(4, 128, 9 * ROWS0)


def dot(a, b, contract, precision=None):
    return lax.dot_general(a, b, (contract, ((), ())), preferred_element_type=F32, precision=precision)


def lane_iota(rows):
    return lax.broadcasted_iota(jnp.int32, (rows, CELLS), 1)


def up_y(block):
    return jnp.where(lane_iota(block.shape[0]) >= 16, pltpu.roll(block, 16, 1), 0.0)


def up_z(block):
    return jnp.where(lane_iota(block.shape[0]) % 16 != 0, pltpu.roll(block, 1, 1), 0.0)


def down_y(block):
    return jnp.where(lane_iota(block.shape[0]) < CELLS - 16, pltpu.roll(block, CELLS - 16, 1), 0.0)


def down_z(block):
    return jnp.where(lane_iota(block.shape[0]) % 16 != 15, pltpu.roll(block, CELLS - 1, 1), 0.0)


def gelu_and_slope(x):
    square = x * x
    t = jnp.tanh(SCALE * (x + 0.044715 * (x * square)))
    half = 0.5 * (1.0 + t)
    slope = half + 0.5 * x * (1.0 - t * t) * (SCALE * (1.0 + 3 * 0.044715 * square))
    return x * half, slope


def fill_permutation(perm_ref):
    z = lax.broadcasted_iota(jnp.int32, (CELLS, CELLS), 0)
    u = lane_iota(CELLS)
    offset = z - 8 * (u % 16)
    for zi in range(9):
        hit = offset == zi - 1
        for y in range(8):
            block = jnp.where(hit & (u // 16 == y), 1.0, 0.0)
            perm_ref[128 * y : 128 * y + 128, 128 * zi : 128 * zi + 128] = block.astype(BF16)


OWN, HALO, ABOVE = 0, 256, 480


def spread_plane(plane_ref, wide_ref, base, x):
    for c in range(4):
        plane = plane_ref[c].astype(F32)
        for y in range(8):
            tile = plane[8 * y : 8 * y + 8]
            wide_ref[base + 8 * c : base + 8 * c + 8, 128 * y : 128 * y + 128] = tile
            if y < 7:
                row = ABOVE + 4 * x + c
                wide_ref[row : row + 1, 128 * y + 128 : 128 * y + 256] = tile[7:8]


def to_cells(wide_ref, perm_ref, start, stop, planes, above, out_ref):
    rows = wide_ref[start:stop, :].astype(BF16)
    upper = lax.broadcasted_iota(jnp.int32, (8, CELLS), 0) < 4
    for first in range(0, 9, 2):
        count = min(2, 9 - first)
        got = dot(rows, perm_ref[:, 128 * first : 128 * (first + count)], ((1,), (0,)))
        for j in range(count):
            lanes = slice(128 * j, 128 * j + 128)
            base = ROWS0 * (first + j)
            for at, x in enumerate(planes):
                out_ref[x, base : base + 32, :] = got[32 * at : 32 * at + 32, lanes].astype(BF16)
            if above:
                for x in range(15):
                    at = 32 * len(planes) + 8 * (x // 2)
                    tile = got[at : at + 8, lanes]
                    tile = jnp.where(upper, tile if x % 2 == 0 else pltpu.roll(tile, 4, 0), 0.0)
                    tile = jnp.concatenate([tile, jnp.zeros((8, CELLS), F32)], axis=0)
                    out_ref[x, base + 32 : base + 48, :] = tile.astype(BF16)


def arrange_kernels(k1_ref, k2_ref, k3_ref, chosen_ref, k1_scratch, w1_ref, w2_ref, w3_ref):
    k1_scratch[...] = k1_ref[...].astype(F32)
    rows = []
    for c in range(4):
        rows += [k1_scratch[:, c, :], jnp.zeros((5, 16), F32)]
    k1 = jnp.concatenate(rows, axis=0).astype(BF16)
    for ry in range(4):
        w1_ref[16 * ry : 16 * ry + 16, :] = dot(k1, chosen_ref[ry], ((0,), (0,))).astype(BF16)
    blank = jnp.zeros((16, 32), BF16)
    for kx in range(3):
        for kz in range(3):
            k = [k2_ref[9 * kx + 3 * ky + kz] for ky in range(3)]
            left = jnp.concatenate([k[1], k[2], blank, blank, k[0]], axis=0)
            right = jnp.concatenate([blank, k[0], k[1], k[2], blank], axis=0)
            base = ROWS1 * (3 * kx + kz)
            w2_ref[base : base + ROWS1, :] = jnp.concatenate([left, right], axis=1)
            base = ROWS2 * (3 * kx + kz)
            for at, ky in enumerate((1, 2, 0)):
                w3_ref[base + 32 * at : base + 32 * at + 32, :] = k3_ref[9 * kx + 3 * ky + kz]


def with_shifts(act, classes, first, ref, x):
    act = act.astype(BF16).astype(F32)
    for zc in range(classes):
        block = act[:, 128 * zc : 128 * zc + 128]
        block = jnp.concatenate([block, up_y(block[first:])], axis=0)
        size = block.shape[0]
        ref[x, size * (zc + 1) : size * (zc + 2), :] = block.astype(BF16)
        if zc == classes - 1:
            ref[x, 0:size, :] = up_z(block).astype(BF16)


def prepare(
    dens_hbm, halo_hbm, k1_hbm, k2_hbm, k3_hbm, chosen_hbm,
    planes_ref, w1_ref, w2_ref, w3_ref,
    dens_ref, halo_ref, k1_ref, k2_ref, k3_ref, chosen_ref, sems, perm_ref, wide_ref, k1_scratch,
):
    sources = (dens_hbm, halo_hbm, k1_hbm, k2_hbm, k3_hbm, chosen_hbm)
    targets = (dens_ref, halo_ref, k1_ref, k2_ref, k3_ref, chosen_ref)
    copies = [pltpu.make_async_copy(a, b, sems.at[i]) for i, (a, b) in enumerate(zip(sources, targets))]
    for copy in copies:
        copy.start()
    wide_ref[ABOVE : ABOVE + 64, 0:128] = jnp.zeros((64, CELLS), F32)
    wide_ref[ABOVE + 56 : ABOVE + 64, 128:1024] = jnp.zeros((8, 896), F32)
    fill_permutation(perm_ref)
    for copy in copies:
        copy.wait()
    for x in range(8):
        spread_plane(dens_ref.at[:, x], wide_ref, OWN + 32 * x, 7 + x)
    for x in range(7):
        spread_plane(halo_ref.at[:, 1 + x], wide_ref, HALO + 32 * x, x)
    to_cells(wide_ref, perm_ref, OWN, ABOVE + 64, [*range(7, 15), *range(7)], True, planes_ref)
    arrange_kernels(k1_ref, k2_ref, k3_ref, chosen_ref, k1_scratch, w1_ref, w2_ref, w3_ref)


def layers(
    planes_ref, w1_ref, w2_ref, w3_ref, cot_ref, chosen_hbm,
    message_ref,
    chosen_ref, sem, cols1_ref, slope1_ref, act1_ref, cols2_ref, slope2_ref, act2_ref, up2_ref, up1_ref, delta1_ref,
    whole_ref,
):
    copy = pltpu.make_async_copy(chosen_hbm, chosen_ref, sem)
    copy.start()
    w1 = w1_ref[...]
    for rx in range(7):
        for kx in range(3):
            for rz in range(4):
                lanes = slice(512 * rx + 128 * rz, 512 * rx + 128 * rz + 128)
                part = planes_ref[2 * rx + kx, 96 * rz : 96 * rz + 144, :]
                cols1_ref[144 * kx : 144 * kx + 144, lanes] = part
        lanes = slice(512 * rx, 512 * rx + 512)
        act, slope1_ref[:, lanes] = gelu_and_slope(dot(w1, cols1_ref[:, lanes], ((1,), (0,))))
        with_shifts(act, 4, 48, act1_ref, rx)
    for rx in range(3):
        for kx in range(3):
            for rz in range(2):
                part = act1_ref[2 * rx + kx, 160 * rz : 160 * rz + 240, :]
                lanes = slice(128 * (2 * rx + rz), 128 * (2 * rx + rz) + 128)
                cols2_ref[240 * kx : 240 * kx + 240, lanes] = part
    act, slope2_ref[...] = gelu_and_slope(dot(w2_ref[...], cols2_ref[...], ((0,), (0,))))
    for rx in range(3):
        with_shifts(act[:, 256 * rx : 256 * rx + 256], 2, 32, act2_ref, rx)
    cols3 = act2_ref[...].reshape(9 * ROWS2, CELLS)
    feat, slope3 = gelu_and_slope(dot(w3_ref[...], cols3, ((0,), (0,))))
    feat = feat.astype(BF16).astype(F32)

    delta3 = (cot_ref[:, 0, :] * slope3).astype(BF16)
    third = jnp.concatenate([dot(delta3, cols3, ((1,), (1,))), jnp.zeros((64, 32), F32)], axis=1)
    up2_ref[...] = dot(w3_ref[...], delta3, ((1,), (0,)))

    def folded2(kx, kz):
        base = ROWS2 * (3 * kx + kz)
        block = up2_ref[base : base + 64, :]
        return jnp.concatenate([block[:32], block[32:] + down_y(up2_ref[base + 64 : base + 96, :])], axis=0)

    delta2 = []
    for kx in range(3):
        for part in (folded2(kx, 1), folded2(kx, 2) + down_z(folded2(kx, 0))):
            at = 128 * len(delta2)
            delta2.append((part * slope2_ref[:, at : at + 128]).astype(BF16))
    delta2 = jnp.concatenate(delta2, axis=1)
    whole2 = dot(delta2, cols2_ref[...], ((1,), (1,)))
    pieces = [None] * 27
    for kx in range(3):
        for kz in range(3):
            base = ROWS1 * (3 * kx + kz)
            for ky in range(3):
                at0 = base + 16 * ((ky - 1) % 5)
                at1 = base + 16 * (ky + 1)
                pieces[9 * kx + 3 * ky + kz] = whole2[:32, at0 : at0 + 16] + whole2[32:, at1 : at1 + 16]
    second = jnp.concatenate(pieces + [jnp.zeros((32, 80), F32)], axis=1)
    up1_ref[...] = dot(w2_ref[...], delta2, ((1,), (0,)))

    def folded1(x, kz, rz):
        total = None
        for kx in range(3):
            rx = x - kx
            if rx % 2 == 0 and 0 <= rx // 2 < 3:
                base = ROWS1 * (3 * kx + kz)
                lanes = slice(128 * (rx + rz), 128 * (rx + rz) + 128)
                part = up1_ref[base : base + ROWS1, lanes]
                total = part if total is None else total + part
        return total

    for x in range(7):
        for zc in range(4):
            if zc % 2 == 0:
                block = folded1(x, 1, zc // 2)
            elif zc == 1:
                block = folded1(x, 2, 0) + folded1(x, 0, 1)
            else:
                block = folded1(x, 2, 1) + down_z(folded1(x, 0, 0))
            block = jnp.concatenate([block[:48], block[48:64] + down_y(block[64:])], axis=0)
            lanes = slice(512 * x + 128 * zc, 512 * x + 128 * zc + 128)
            delta1_ref[:, lanes] = (block * slope1_ref[:, lanes]).astype(BF16)
    whole1 = dot(delta1_ref[...], cols1_ref[...], ((1,), (1,)))
    parts = []
    for _ in range(3):
        parts.append(whole1.astype(BF16))
        whole1 = whole1 - parts[-1].astype(F32)
    first = None
    copy.wait()
    for ry in range(4):
        rows = jnp.concatenate([part[16 * ry : 16 * ry + 16] for part in parts], axis=0)
        got = dot(rows, chosen_ref[ry], ((1,), (1,)))
        for at in (0, 16, 32):
            first = got[at : at + 16] if first is None else first + got[at : at + 16]

    def put(row, value):
        whole_ref[pl.ds(row, 16, stride=48), :] = value

    for x in range(4):
        for r in range(7):
            put(8 * x + r, third[16 * x : 16 * x + 16, 128 * r : 128 * r + 128])
        put(8 * x + 7, feat[16 * x : 16 * x + 16])
    for h in range(2):
        for r in range(4):
            value = second[16 * h : 16 * h + 16, 128 * r : 128 * r + 128]
            if r == 3:
                value = jnp.where(lane_iota(16) < 64, value, pltpu.roll(first, 64, 1) if h == 0 else first)
            upper = value.astype(BF16).astype(F32)
            put(32 + 4 * h + r, upper)
            put(40 + 4 * h + r, value - upper)
    message_ref[...] = whole_ref[...].astype(BF16)


def passed_along(block, axis, distance):
    devices = range(lax.axis_size(axis))
    route = [(i, i + distance) for i in devices if i + distance in devices]
    return lax.ppermute(block, axis, route)


def turn(cot_hbm, out_ref, cot_ref, sem):
    copy = pltpu.make_async_copy(cot_hbm, cot_ref, sem)
    copy.start()
    copy.wait()
    out_ref[:, 0, :] = cot_ref[...].astype(F32).T


def regroup(got_ref, message_ref, whole_ref):
    whole_ref[...] = got_ref[...].astype(F32)
    total = whole_ref[0:48, :]
    for j in range(1, 16):
        total = total + whole_ref[48 * j : 48 * j + 48, :]
    shared = total[32:40] + total[40:48]
    for x in range(4):
        sums = jnp.concatenate([total[8 * x : 8 * x + 8], shared], axis=0).astype(BF16)
        feat = whole_ref[pl.ds(8 * x + 7, 16, stride=48), :].astype(BF16)
        for dp in range(4):
            base = 128 * dp + 32 * x
            message_ref[base : base + 16, :] = sums
            message_ref[base + 16 : base + 32, :] = feat


def total_of(got_ref):
    total = got_ref[0:16, :].astype(F32)
    for j in range(1, 16):
        total = total + got_ref[32 * j : 32 * j + 16, :].astype(F32)
    return total


def share(got_ref, message_ref):
    total = total_of(got_ref)[8:]
    for j in range(16):
        message_ref[8 * j : 8 * j + 8, :] = total


def settle(dp_ref, got_ref, feat_ref, third_ref):
    base = pl.multiple_of(128 * dp_ref[0], 128)
    feat = [got_ref[pl.ds(base + 32 * x + 16, 16), :].astype(F32) for x in range(4)]
    feat_ref[...] = jnp.concatenate(feat, axis=0).T.astype(BF16)
    total = total_of(got_ref)[:8]
    turned = [total] + [pltpu.roll(total, 128 - 32 * q, 1) for q in range(1, 4)]
    for kx in range(3):
        for kz in range(3):
            for at, ky in enumerate((1, 2, 0)):
                b = 9 * kx + 3 * kz + at
                third_ref[9 * kx + 3 * ky + kz] = turned[b % 4][b // 4 : b // 4 + 1, :32]


def unpack(got_ref, first_ref, second_ref):
    halves = []
    for h in range(2):
        halves.append(jnp.concatenate([got_ref[pl.ds(4 * h + r, 16, stride=8), :] for r in range(4)], axis=1))
    both = jnp.concatenate(halves, axis=0).T
    second_ref[...] = both[:432]
    for c in range(4):
        h, q = c // 2, c % 2
        first_ref[:, c, :] = both[448 + 32 * q : 475 + 32 * q, 16 * h : 16 * h + 16]


def vmem(*shape, dtype=F32):
    return pltpu.VMEM(shape, dtype)


def call(kernel, out_shape, scratch=(), limit=8, **options):
    return pl.pallas_call(
        kernel,
        out_shape=out_shape,
        scratch_shapes=list(scratch),
        compiler_params=pltpu.CompilerParams(vmem_limit_bytes=limit * 1024 * 1024),
        **options,
    )


IN_HBM = pl.BlockSpec(memory_space=pltpu.HBM)
IN_VMEM = pl.BlockSpec(memory_space=pltpu.VMEM)


def in_hbm(array):
    return pltpu.with_memory_space_constraint(array, pltpu.HBM)


def in_vmem(array):
    return pltpu.with_memory_space_constraint(array, pltpu.VMEM)


def local_message(halo, dens, k1, k2, k3, cot):
    chosen = jnp.asarray(first_selection(), BF16)
    k1 = jnp.transpose(k1, (2, 3, 4, 1, 0)).reshape(27, 4, 16)
    k2 = jnp.transpose(k2, (2, 3, 4, 1, 0)).reshape(27, 16, 32)
    k3 = jnp.transpose(k3, (2, 3, 4, 1, 0)).reshape(27, 32, 64)
    arguments = (dens, halo, k1, k2, k3, chosen)
    pinned = [array if array is halo else in_hbm(array) for array in arguments]
    prepared = call(
        prepare,
        (
            vmem(15, 9 * ROWS0, CELLS, dtype=BF16),
            vmem(64, 9 * ROWS0, dtype=BF16),
            vmem(9 * ROWS1, 64, dtype=BF16),
            vmem(9 * ROWS2, 64, dtype=BF16),
        ),
        [
            *(vmem(*array.shape, dtype=BF16) for array in arguments),
            pltpu.SemaphoreType.DMA((6,)),
            vmem(1024, 1152, dtype=BF16),
            vmem(ABOVE + 64, 1024),
            vmem(27, 4, 16),
        ],
        20,
        in_specs=[IN_HBM, pl.BlockSpec(memory_space=pl.ANY)] + [IN_HBM] * 4,
        out_specs=(IN_VMEM,) * 4,
    )(*pinned)
    return call(
        layers,
        jax.ShapeDtypeStruct((768, CELLS), BF16),
        [
            vmem(*chosen.shape, dtype=BF16),
            pltpu.SemaphoreType.DMA,
            vmem(9 * ROWS0, 3584, dtype=BF16),
            vmem(64, 3584),
            vmem(7, 5 * ROWS1, CELLS, dtype=BF16),
            vmem(9 * ROWS1, 768, dtype=BF16),
            vmem(64, 768),
            vmem(3, 3 * ROWS2, CELLS, dtype=BF16),
            vmem(9 * ROWS2, CELLS),
            vmem(9 * ROWS1, 768),
            vmem(64, 3584, dtype=BF16),
            vmem(768, CELLS),
        ],
        26,
        in_specs=[IN_VMEM] * 5 + [IN_HBM],
    )(*map(in_vmem, prepared), cot, in_hbm(chosen))


def exchanged(rows, axes):
    size = lax.axis_size(axes)
    blocks = rows.reshape(size, rows.shape[0] // size, CELLS)
    return lax.all_to_all(blocks, axes, 0, 0, tiled=True).reshape(rows.shape)


def shards(density_cubes, first_kernel, second_kernel, third_kernel, cotangent):
    shape = jax.ShapeDtypeStruct
    dens = density_cubes[0]
    halo = passed_along(dens, SPACE, 1)
    cot = jnp.transpose(cotangent, (0, 1, 3, 4, 2)).reshape(CELLS, 64)
    scratch = [vmem(CELLS, 64, dtype=BF16), pltpu.SemaphoreType.DMA]
    cot = call(turn, shape((64, 1, CELLS), F32), scratch, in_specs=[IN_HBM])(in_hbm(cot))
    cot = lax.all_to_all(cot, SPACE, 0, 0, tiled=True)
    message = local_message(halo, dens, first_kernel, second_kernel, third_kernel, cot)
    got = exchanged(message, NEAR)
    got = exchanged(call(regroup, shape((512, CELLS), BF16), [vmem(768, CELLS)])(got), FAR)
    both = exchanged(call(share, shape((CELLS, CELLS), F32))(got), NEAR)
    specs = [pl.BlockSpec(memory_space=pltpu.SMEM), pl.BlockSpec()]
    dp = lax.axis_index("dp").reshape(1)
    feat, third = call(settle, (shape((CELLS, 64), BF16), shape((27, 1, 32), F32)), in_specs=specs)(dp, got)
    first, second = call(unpack, (shape((27, 4, 16), F32), shape((432, 32), F32)))(both)
    features = jnp.transpose(feat.reshape(1, 1, 8, 16, 64), (0, 1, 4, 2, 3))
    first_grad = jnp.transpose(first.reshape(3, 3, 3, 4, 16), (4, 3, 0, 1, 2))
    second_grad = jnp.transpose(second.reshape(3, 3, 3, 16, 32), (4, 3, 0, 1, 2))
    third_grad = jnp.transpose(third.reshape(3, 3, 3, 1, 32), (3, 4, 0, 1, 2))
    return (features, first_grad, second_grad, third_grad)


def solution(mesh):
    mesh = jax.sharding.Mesh(mesh.devices.reshape(4, 4, 2, 4, 2), ("dp",) + SPACE)
    in_specs = (
        P("dp", None, SPACE, None, None),
        P(),
        P(),
        P(),
        P("dp", SPACE, None, None, None),
    )
    out_specs = (P("dp", SPACE, None, None, None), P(), P(), P(SPACE, None, None, None, None))
    return jax.shard_map(shards, mesh=mesh, in_specs=in_specs, out_specs=out_specs, check_vma=False)
```

time: 768 us -> 68.5 us (0.09); the launches traced: 757 us -> 68.1 us
  waiting for transfers between devices: 316 us -> 9.65 us
  matrix products: 130 us -> 0 us
  local copies, waits for them, and re-layouts: 123 us -> 0 us
  blocking collectives: 105 us -> 27 us
  other arithmetic: 30.8 us -> 0 us
  starting transfers between devices: 37 us -> 18.8 us
  between operations: 14.9 us -> 0.69 us
  Pallas kernels: 0 us -> 12 us
    unnamed x2 -> x0, waiting for transfers between devices: 312 us -> none
    psum x2 -> x0, blocking collectives: 105 us -> none  [the longest x1 88.7 us: shards(): lax.psum((local_first, local_second), ('dp', 'space'))]
    transpose x3 -> x0, matrix products: 104 us -> none  [kernel_gradient(): return jnp.transpose(result, (1, 0, 2, 3, 4))]
    concatenate x7 -> x0, local copies, waits for them, and re-layouts: 55.4 us -> none  [the longest x3 41.8 us: shards(): widened_cubes = jnp.concatenate([lower_plane, density_cubes], axis=2)]
    conv_general_dilated x21 -> x0, local copies, waits for them, and re-layouts: 32.9 us -> none  [the longest x9 22.9 us: convolve(): lax.conv_general_dilated(inputs, kernel, (2, 2, 2), padding, dimension_nu...]
    all_to_all x0 -> x2, blocking collectives: none -> 27 us  [exchanged(): return lax.all_to_all(blocks, axes, 0, 0, tiled=True).reshape(rows.shape)]
    conv_general_dilated x5 -> x0, matrix products: 26 us -> none  [the longest x3 21.8 us: convolve(): lax.conv_general_dilated(inputs, kernel, (2, 2, 2), padding, dimension_nu...]
    unnamed x53 -> x0, local copies, waits for them, and re-layouts: 19.9 us -> none
  transfers between devices with their start and end apart: 8 -> 3, of which waited for: 3 -> 2; matrix products, arithmetic and copies ran while one was open for 30% -> 0% of each run, Pallas kernels for 0% -> 8%
where the time goes in v1:
time: 68.5 us; the launch traced here: 68.1 us
  blocking collectives  27 us (39%)
  starting transfers between devices  18.8 us (27%)
  Pallas kernels  12 us (18%)
  waiting for transfers between devices  9.65 us (14%)
  between operations  0.69 us (1%)
    all_to_all x2, blocking collectives, exchanged(): return lax.all_to_all(blocks, axes, 0, 0, tiled=True).reshape(rows.shape)  27 us
    all_to_all x1, starting transfers between devices, shards(): cot = lax.all_to_all(cot, SPACE, 0, 0, tiled=True)  8.67 us
    all_to_all x1, starting transfers between devices, exchanged(): return lax.all_to_all(blocks, axes, 0, 0, tiled=True).reshape(rows.shape)  5.51 us
    all_to_all x1, waiting for transfers between devices, exchanged(): return lax.all_to_all(blocks, axes, 0, 0, tiled=True).reshape(rows.shape)  5.17 us
    pallas_call x1, Pallas kernels, local_message(): call(layers, jax.ShapeDtypeStruct((768, CELLS), BF16), [vmem(*chosen.shap...  4.99 us
    ppermute x1, starting transfers between devices, passed_along(): return lax.ppermute(block, axis, route)  4.6 us
    all_to_all x1, waiting for transfers between devices, shards(): cot = lax.all_to_all(cot, SPACE, 0, 0, tiled=True)  4.47 us
    pallas_call x1, Pallas kernels, local_message(): call(prepare, (vmem(15, 9 * ROWS0, CELLS, dtype=BF16), vmem(64, 9 * ROWS0...  3.22 us
  transfers between devices with their start and end apart: 3, of which 2 were waited for; matrix products, arithmetic and copies ran while one was open for 0% of the time, Pallas kernels for 8%

profile of v1, /device:TPU:1, one launch (start us, length us, event | category | flops | bytes accessed | tf_op | source)
XLA Modules:
  0.0 68.1 jit_solution(4405863612067486068)
XLA Ops:
  0.6 4.6 %collective-permute-start = (bf16[4,8,64,128]{3,2,1,0:T(8,128)(2,1)}, bf16[4,8,64,128]{3,2,1,0:T(8,128)(2,1)S(1)}, u32[]{:S(2)}, u32[]{:S(2)}) collective-permute-start(bf16[4,8,64,128]{3,2,1,0:T(8,128)(2,1)} %bitcast.38), channel_id=1, source_target_pairs={{0,1},{1,2},{2,3},{3,4},{4,5},{5,6},{6,7},{7,8},{8,9},{9,10},{10,1... | collective-permute-start | bytes 1572872 | tf_op jit(solution)/shard_map/ppermute | solution.py:281
  5.2 1.5 %shard_map.94 = f32[64,1,128]{2,1,0:T(1,128)} custom-call(bf16[128,64]{1,0:T(8,128)(2,1)} %bitcast.42), custom_call_target="tpu_custom_call" | custom-call | tf_op jit(solution)/shard_map/pallas_call | solution.py:429
  6.7 8.7 %all-to-all-start = ((f32[64,1,128]{2,1,0:T(1,128)}), f32[64,1,128]{2,1,0:T(1,128)S(1)}, u32[]{:S(2)}, u32[]{:S(2)}) async-start(f32[64,1,128]{2,1,0:T(1,128)} %shard_map.94), calls=%async_computation | async-start | bytes 65536 | tf_op jit(solution)/shard_map/all_to_all | solution.py:430
  15.4 0.0 collective-permute-done.halo_hbm
  15.4 3.2 %shard_map.93 = (bf16[15,432,128]{2,1,0:T(8,128)(2,1)S(1)}, bf16[64,432]{1,0:T(8,128)(2,1)S(1)}, bf16[720,64]{1,0:T(8,128)(2,1)S(1)}, bf16[864,64]{1,0:T(8,128)(2,1)S(1)}) custom-call(bf16[4,8,64,128]{3,2,1,0:T(8,128)(2,1)} %bitcast.39, bf16[4,8,64,128]{3,2,1,0:T(8,128)(2,1)S(1)} %collective-permute-done.halo_hbm, bf16[27,4,16]{2,1,0:T(4,128)(2,1)} %bitcast.43, ...), custom_call_target="tpu_custom_call" | custom-call | tf_op jit(solution)/shard_map/pallas_call | solution.py:376
  18.6 4.5 %all-to-all-done.cot_ref = f32[64,1,128]{2,1,0:T(1,128)S(1)} async-done(((f32[64,1,128]{2,1,0:T(1,128)}), f32[64,1,128]{2,1,0:T(1,128)S(1)}, u32[]{:S(2)}, u32[]{:S(2)}) %all-to-all-start) | async-done | bytes 32800 | tf_op jit(solution)/shard_map/all_to_all | solution.py:430
  23.1 5.0 %shard_map.95 = bf16[768,128]{1,0:T(8,128)(2,1)S(1)} custom-call(bf16[15,432,128]{2,1,0:T(8,128)(2,1)S(1)} %get-tuple-element.12.planes_ref, bf16[64,432]{1,0:T(8,128)(2,1)S(1)} %get-tuple-element.13.w1_ref, bf16[720,64]{1,0:T(8,128)(2,1)S(1)} %get-tuple-element.14.w2_ref, bf16[864,64]{1,0:T(8,128)(2,1)S(1)} %get-tuple-element.15.w3_ref, ...), custom_call_target="tpu_custom_call" | custom-call | tf_op jit(solution)/shard_map/pallas_call | solution.py:395
  28.1 9.8 %all_to_all.20 = bf16[16,48,128]{2,1,0:T(8,128)(2,1)S(1)} all-to-all(bf16[16,48,128]{2,1,0:T(8,128)(2,1)S(1)} %bitcast.34), channel_id=1, replica_groups=mesh['dp'=4,'x'=4,'z'=2,'y'=4,'core'=2] {'z','y','core'}, dimensions={0} | all-to-all | bytes 393216 | tf_op jit(solution)/shard_map/all_to_all | solution.py:420
  37.9 0.1 shard_map.96
  38.0 17.2 %all_to_all.21 = bf16[16,32,128]{2,1,0:T(8,128)(2,1)S(1)} all-to-all(bf16[16,32,128]{2,1,0:T(8,128)(2,1)S(1)} %bitcast.36), channel_id=1, replica_groups=mesh['dp'=4,'x'=4,'z'=2,'y'=4,'core'=2] {'dp','x'}, dimensions={0} | all-to-all | bytes 262144 | tf_op jit(solution)/shard_map/all_to_all | solution.py:420
  55.2 0.7 shard_map.98
  55.8 5.5 %all-to-all-start.3 = ((f32[16,8,128]{2,1,0:T(8,128)}), f32[16,8,128]{2,1,0:T(8,128)S(1)}, u32[]{:S(2)}, u32[]{:S(2)}) async-start(f32[16,8,128]{2,1,0:T(8,128)} %bitcast.16), calls=%async_computation.3 | async-start | bytes 131072 | tf_op jit(solution)/shard_map/all_to_all | solution.py:420
  61.3 0.7 %shard_map.97 = (bf16[128,64]{1,0:T(8,128)(2,1)}, f32[27,1,32]{2,1,0:T(1,128)}) custom-call(s32[1]{0:T(128)} %bitcast.dp_ref, bf16[512,128]{1,0:T(8,128)(2,1)S(1)} %bitcast.33), custom_call_target="tpu_custom_call" | custom-call | tf_op jit(solution)/shard_map/pallas_call | solution.py:437
  62.0 5.2 %all-to-all-done.3 = f32[16,8,128]{2,1,0:T(8,128)S(1)} async-done(((f32[16,8,128]{2,1,0:T(8,128)}), f32[16,8,128]{2,1,0:T(8,128)S(1)}, u32[]{:S(2)}, u32[]{:S(2)}) %all-to-all-start.3) | async-done | bytes 65568 | tf_op jit(solution)/shard_map/all_to_all | solution.py:420
  67.2 0.9 %shard_map.99 = (f32[27,4,16]{2,1,0:T(4,128)}, f32[432,32]{1,0:T(8,128)}) custom-call(f32[128,128]{1,0:T(8,128)S(1)} %bitcast.37), custom_call_target="tpu_custom_call" | custom-call | tf_op jit(solution)/shard_map/pallas_call | solution.py:438
Async XLA Ops:
  0.6 14.8 %collective-permute-start = (bf16[4,8,64,128]{3,2,1,0:T(8,128)(2,1)}, bf16[4,8,64,128]{3,2,1,0:T(8,128)(2,1)S(1)}, u32[]{:S(2)}, u32[]{:S(2)}) collective-permute-start(bf16[4,8,64,128]{3,2,1,0:T(8,128)(2,1)} %bitcast.38), channel_id=1, source_target_pairs={{0,1},{1,2},{2,3},{3,4},{4,5},{5,6},{6,7},{7,8},{8,9},{9,10},{10,1... | collective-permute-start | bytes 1572872 | tf_op jit(solution)/shard_map/ppermute | solution.py:281
  6.7 16.4 %all-to-all-start = ((f32[64,1,128]{2,1,0:T(1,128)}), f32[64,1,128]{2,1,0:T(1,128)S(1)}, u32[]{:S(2)}, u32[]{:S(2)}) async-start(f32[64,1,128]{2,1,0:T(1,128)} %shard_map.94), calls=%async_computation | async-start | bytes 65536 | tf_op jit(solution)/shard_map/all_to_all | solution.py:430
  55.8 11.4 %all-to-all-start.3 = ((f32[16,8,128]{2,1,0:T(8,128)}), f32[16,8,128]{2,1,0:T(8,128)S(1)}, u32[]{:S(2)}, u32[]{:S(2)}) async-start(f32[16,8,128]{2,1,0:T(8,128)} %bitcast.16), calls=%async_computation.3 | async-start | bytes 131072 | tf_op jit(solution)/shard_map/all_to_all | solution.py:420

commit v2 on v1

--- a/solution.py
+++ b/solution.py
@@ -109,7 +109,7 @@
                     out_ref[x, base + 32 : base + 48, :] = tile.astype(BF16)
 
 
-def arrange_kernels(k1_ref, k2_ref, k3_ref, chosen_ref, k1_scratch, w1_ref, w2_ref, w3_ref):
+def arrange_kernels(k1_ref, k2_ref, k3_ref, chosen_ref, k1_scratch, w1_ref, w2_ref, w3_ref, w2t_ref, w3t_ref):
     k1_scratch[...] = k1_ref[...].astype(F32)
     rows = []
     for c in range(4):
@@ -128,6 +128,8 @@
             base = ROWS2 * (3 * kx + kz)
             for at, ky in enumerate((1, 2, 0)):
                 w3_ref[base + 32 * at : base + 32 * at + 32, :] = k3_ref[9 * kx + 3 * ky + kz]
+    w2t_ref[...] = w2_ref[...].astype(F32).T.astype(BF16)
+    w3t_ref[...] = w3_ref[...].astype(F32).T.astype(BF16)
 
 
 def with_shifts(act, classes, first, ref, x):
@@ -142,30 +144,31 @@
 
 
 def prepare(
-    dens_hbm, halo_hbm, k1_hbm, k2_hbm, k3_hbm, chosen_hbm,
-    planes_ref, w1_ref, w2_ref, w3_ref,
-    dens_ref, halo_ref, k1_ref, k2_ref, k3_ref, chosen_ref, sems, perm_ref, wide_ref, k1_scratch,
+    dens_ref, halo_any, k1_hbm, k2_hbm, k3_hbm, chosen_hbm,
+    planes_ref, w1_ref, w2_ref, w3_ref, w2t_ref, w3t_ref,
+    halo_ref, k1_ref, k2_ref, k3_ref, chosen_ref, sems, perm_ref, wide_ref, k1_scratch,
 ):
-    sources = (dens_hbm, halo_hbm, k1_hbm, k2_hbm, k3_hbm, chosen_hbm)
-    targets = (dens_ref, halo_ref, k1_ref, k2_ref, k3_ref, chosen_ref)
+    sources = (halo_any, k1_hbm, k2_hbm, k3_hbm, chosen_hbm)
+    targets = (halo_ref, k1_ref, k2_ref, k3_ref, chosen_ref)
     copies = [pltpu.make_async_copy(a, b, sems.at[i]) for i, (a, b) in enumerate(zip(sources, targets))]
     for copy in copies:
         copy.start()
     wide_ref[ABOVE : ABOVE + 64, 0:128] = jnp.zeros((64, CELLS), F32)
     wide_ref[ABOVE + 56 : ABOVE + 64, 128:1024] = jnp.zeros((8, 896), F32)
     fill_permutation(perm_ref)
-    for copy in copies:
-        copy.wait()
     for x in range(8):
         spread_plane(dens_ref.at[:, x], wide_ref, OWN + 32 * x, 7 + x)
+    copies[0].wait()
     for x in range(7):
         spread_plane(halo_ref.at[:, 1 + x], wide_ref, HALO + 32 * x, x)
     to_cells(wide_ref, perm_ref, OWN, ABOVE + 64, [*range(7, 15), *range(7)], True, planes_ref)
-    arrange_kernels(k1_ref, k2_ref, k3_ref, chosen_ref, k1_scratch, w1_ref, w2_ref, w3_ref)
+    for copy in copies[1:]:
+        copy.wait()
+    arrange_kernels(k1_ref, k2_ref, k3_ref, chosen_ref, k1_scratch, w1_ref, w2_ref, w3_ref, w2t_ref, w3t_ref)
 
 
 def layers(
-    planes_ref, w1_ref, w2_ref, w3_ref, cot_ref, chosen_hbm,
+    planes_ref, w1_ref, w2_ref, w3_ref, w2t_ref, w3t_ref, cot_ref, chosen_hbm,
     message_ref,
     chosen_ref, sem, cols1_ref, slope1_ref, act1_ref, cols2_ref, slope2_ref, act2_ref, up2_ref, up1_ref, delta1_ref,
     whole_ref,
@@ -188,11 +191,11 @@
                 part = act1_ref[2 * rx + kx, 160 * rz : 160 * rz + 240, :]
                 lanes = slice(128 * (2 * rx + rz), 128 * (2 * rx + rz) + 128)
                 cols2_ref[240 * kx : 240 * kx + 240, lanes] = part
-    act, slope2_ref[...] = gelu_and_slope(dot(w2_ref[...], cols2_ref[...], ((0,), (0,))))
+    act, slope2_ref[...] = gelu_and_slope(dot(w2t_ref[...], cols2_ref[...], ((1,), (0,))))
     for rx in range(3):
         with_shifts(act[:, 256 * rx : 256 * rx + 256], 2, 32, act2_ref, rx)
     cols3 = act2_ref[...].reshape(9 * ROWS2, CELLS)
-    feat, slope3 = gelu_and_slope(dot(w3_ref[...], cols3, ((0,), (0,))))
+    feat, slope3 = gelu_and_slope(dot(w3t_ref[...], cols3, ((1,), (0,))))
     feat = feat.astype(BF16).astype(F32)
 
     delta3 = (cot_ref[:, 0, :] * slope3).astype(BF16)
@@ -210,16 +213,16 @@
             at = 128 * len(delta2)
             delta2.append((part * slope2_ref[:, at : at + 128]).astype(BF16))
     delta2 = jnp.concatenate(delta2, axis=1)
-    whole2 = dot(delta2, cols2_ref[...], ((1,), (1,)))
-    pieces = [None] * 27
+    whole2 = [dot(cols2_ref[...], delta2[32 * ry : 32 * ry + 32], ((1,), (1,))) for ry in range(2)]
+    pieces = []
     for kx in range(3):
-        for kz in range(3):
-            base = ROWS1 * (3 * kx + kz)
-            for ky in range(3):
+        for ky in range(3):
+            for kz in range(3):
+                base = ROWS1 * (3 * kx + kz)
                 at0 = base + 16 * ((ky - 1) % 5)
                 at1 = base + 16 * (ky + 1)
-                pieces[9 * kx + 3 * ky + kz] = whole2[:32, at0 : at0 + 16] + whole2[32:, at1 : at1 + 16]
-    second = jnp.concatenate(pieces + [jnp.zeros((32, 80), F32)], axis=1)
+                pieces.append(whole2[0][at0 : at0 + 16] + whole2[1][at1 : at1 + 16])
+    second = jnp.concatenate(pieces + [jnp.zeros((80, 32), F32)], axis=0).T
     up1_ref[...] = dot(w2_ref[...], delta2, ((1,), (0,)))
 
     def folded1(x, kz, rz):
@@ -272,7 +275,7 @@
             upper = value.astype(BF16).astype(F32)
             put(32 + 4 * h + r, upper)
             put(40 + 4 * h + r, value - upper)
-    message_ref[...] = whole_ref[...].astype(BF16)
+    message_ref[...] = whole_ref[0:768, :].astype(BF16)
 
 
 def passed_along(block, axis, distance):
@@ -281,15 +284,17 @@
     return lax.ppermute(block, axis, route)
 
 
-def turn(cot_hbm, out_ref, cot_ref, sem):
-    copy = pltpu.make_async_copy(cot_hbm, cot_ref, sem)
-    copy.start()
-    copy.wait()
+def fetch(cot_hbm, dens_hbm, out_ref, dens_ref, cot_ref, sems):
+    copies = [pltpu.make_async_copy(cot_hbm, cot_ref, sems.at[0]), pltpu.make_async_copy(dens_hbm, dens_ref, sems.at[1])]
+    for copy in copies:
+        copy.start()
+    copies[0].wait()
     out_ref[:, 0, :] = cot_ref[...].astype(F32).T
+    copies[1].wait()
 
 
 def regroup(got_ref, message_ref, whole_ref):
-    whole_ref[...] = got_ref[...].astype(F32)
+    whole_ref[0:768, :] = got_ref[...].astype(F32)
     total = whole_ref[0:48, :]
     for j in range(1, 16):
         total = total + whole_ref[48 * j : 48 * j + 48, :]
@@ -316,7 +321,8 @@
         message_ref[8 * j : 8 * j + 8, :] = total
 
 
-def settle(dp_ref, got_ref, feat_ref, third_ref):
+def finish(dp_ref, got_ref, shared_ref, feat_ref, first_ref, second_ref, third_ref, whole_ref):
+    whole_ref[0:CELLS, :] = shared_ref[...]
     base = pl.multiple_of(128 * dp_ref[0], 128)
     feat = [got_ref[pl.ds(base + 32 * x + 16, 16), :].astype(F32) for x in range(4)]
     feat_ref[...] = jnp.concatenate(feat, axis=0).T.astype(BF16)
@@ -327,12 +333,9 @@
             for at, ky in enumerate((1, 2, 0)):
                 b = 9 * kx + 3 * kz + at
                 third_ref[9 * kx + 3 * ky + kz] = turned[b % 4][b // 4 : b // 4 + 1, :32]
-
-
-def unpack(got_ref, first_ref, second_ref):
     halves = []
     for h in range(2):
-        halves.append(jnp.concatenate([got_ref[pl.ds(4 * h + r, 16, stride=8), :] for r in range(4)], axis=1))
+        halves.append(jnp.concatenate([whole_ref[pl.ds(4 * h + r, 16, stride=8), :] for r in range(4)], axis=1))
     both = jnp.concatenate(halves, axis=0).T
     second_ref[...] = both[:432]
     for c in range(4):
@@ -366,13 +369,22 @@
     return pltpu.with_memory_space_constraint(array, pltpu.VMEM)
 
 
+def fetched(cot, dens):
+    return call(
+        fetch,
+        (jax.ShapeDtypeStruct((64, 1, CELLS), F32), vmem(*dens.shape, dtype=BF16)),
+        [vmem(CELLS, 64, dtype=BF16), pltpu.SemaphoreType.DMA((2,))],
+        in_specs=[IN_HBM] * 2,
+        out_specs=(IN_VMEM,) * 2,
+    )(in_hbm(cot), in_hbm(dens))
+
+
 def local_message(halo, dens, k1, k2, k3, cot):
     chosen = jnp.asarray(first_selection(), BF16)
     k1 = jnp.transpose(k1, (2, 3, 4, 1, 0)).reshape(27, 4, 16)
     k2 = jnp.transpose(k2, (2, 3, 4, 1, 0)).reshape(27, 16, 32)
     k3 = jnp.transpose(k3, (2, 3, 4, 1, 0)).reshape(27, 32, 64)
-    arguments = (dens, halo, k1, k2, k3, chosen)
-    pinned = [array if array is halo else in_hbm(array) for array in arguments]
+    arguments = (halo, k1, k2, k3, chosen)
     prepared = call(
         prepare,
         (
@@ -380,18 +392,20 @@
             vmem(64, 9 * ROWS0, dtype=BF16),
             vmem(9 * ROWS1, 64, dtype=BF16),
             vmem(9 * ROWS2, 64, dtype=BF16),
+            vmem(64, 9 * ROWS1, dtype=BF16),
+            vmem(64, 9 * ROWS2, dtype=BF16),
         ),
         [
             *(vmem(*array.shape, dtype=BF16) for array in arguments),
-            pltpu.SemaphoreType.DMA((6,)),
+            pltpu.SemaphoreType.DMA((5,)),
             vmem(1024, 1152, dtype=BF16),
             vmem(ABOVE + 64, 1024),
             vmem(27, 4, 16),
         ],
         20,
-        in_specs=[IN_HBM, pl.BlockSpec(memory_space=pl.ANY)] + [IN_HBM] * 4,
-        out_specs=(IN_VMEM,) * 4,
-    )(*pinned)
+        in_specs=[IN_VMEM, pl.BlockSpec(memory_space=pl.ANY)] + [IN_HBM] * 4,
+        out_specs=(IN_VMEM,) * 6,
+    )(in_vmem(dens), halo, *map(in_hbm, arguments[1:]))
     return call(
         layers,
         jax.ShapeDtypeStruct((768, CELLS), BF16),
@@ -407,10 +421,10 @@
             vmem(9 * ROWS2, CELLS),
             vmem(9 * ROWS1, 768),
             vmem(64, 3584, dtype=BF16),
-            vmem(768, CELLS),
+            vmem(816, CELLS),
         ],
         26,
-        in_specs=[IN_VMEM] * 5 + [IN_HBM],
+        in_specs=[IN_VMEM] * 7 + [IN_HBM],
     )(*map(in_vmem, prepared), cot, in_hbm(chosen))
 
 
@@ -425,17 +439,16 @@
     dens = density_cubes[0]
     halo = passed_along(dens, SPACE, 1)
     cot = jnp.transpose(cotangent, (0, 1, 3, 4, 2)).reshape(CELLS, 64)
-    scratch = [vmem(CELLS, 64, dtype=BF16), pltpu.SemaphoreType.DMA]
-    cot = call(turn, shape((64, 1, CELLS), F32), scratch, in_specs=[IN_HBM])(in_hbm(cot))
+    cot, dens = fetched(cot, dens)
     cot = lax.all_to_all(cot, SPACE, 0, 0, tiled=True)
     message = local_message(halo, dens, first_kernel, second_kernel, third_kernel, cot)
+    message, dp = lax.optimization_barrier((message, lax.axis_index("dp").reshape(1)))
     got = exchanged(message, NEAR)
-    got = exchanged(call(regroup, shape((512, CELLS), BF16), [vmem(768, CELLS)])(got), FAR)
+    got = exchanged(call(regroup, shape((512, CELLS), BF16), [vmem(816, CELLS)])(got), FAR)
     both = exchanged(call(share, shape((CELLS, CELLS), F32))(got), NEAR)
-    specs = [pl.BlockSpec(memory_space=pltpu.SMEM), pl.BlockSpec()]
-    dp = lax.axis_index("dp").reshape(1)
-    feat, third = call(settle, (shape((CELLS, 64), BF16), shape((27, 1, 32), F32)), in_specs=specs)(dp, got)
-    first, second = call(unpack, (shape((27, 4, 16), F32), shape((432, 32), F32)))(both)
+    outs = (shape((CELLS, 64), BF16), shape((27, 4, 16), F32), shape((432, 32), F32), shape((27, 1, 32), F32))
+    specs = [pl.BlockSpec(memory_space=pltpu.SMEM), pl.BlockSpec(), pl.BlockSpec()]
+    feat, first, second, third = call(finish, outs, [vmem(136, CELLS)], in_specs=specs)(dp, got, both)
     features = jnp.transpose(feat.reshape(1, 1, 8, 16, 64), (0, 1, 4, 2, 3))
     first_grad = jnp.transpose(first.reshape(3, 3, 3, 4, 16), (4, 3, 0, 1, 2))
     second_grad = jnp.transpose(second.reshape(3, 3, 3, 16, 32), (4, 3, 0, 1, 2))

time: 68.5 us -> 67 us (0.978)
  blocking collectives: 27 us -> 37.7 us
  starting transfers between devices: 18.8 us -> 13.3 us
  waiting for transfers between devices: 9.65 us -> 5.09 us
  Pallas kernels: 12 us -> 9.97 us
    all_to_all x2 -> x3, blocking collectives: 27 us -> 37.7 us  [exchanged(): return lax.all_to_all(blocks, axes, 0, 0, tiled=True).reshape(rows.shape)]
    all_to_all x1 -> x0, starting transfers between devices: 5.51 us -> none  [exchanged(): return lax.all_to_all(blocks, axes, 0, 0, tiled=True).reshape(rows.shape)]
    all_to_all x1 -> x0, waiting for transfers between devices: 5.17 us -> none  [exchanged(): return lax.all_to_all(blocks, axes, 0, 0, tiled=True).reshape(rows.shape)]
    pallas_call x4 -> x3, Pallas kernels: 3.12 us -> 2.78 us  [the longest x1 1.73 us: fetched(): call(fetch, (jax.ShapeDtypeStruct((64, 1, CELLS), F32), vmem(*dens.shape,...]
  transfers between devices with their start and end apart: 3 -> 2, of which waited for: 2 -> 1; matrix products, arithmetic and copies ran while one was open for 0% -> 0% of each run, Pallas kernels for 8% -> 6%
where the time goes in v2:
time: 67 us; the launch traced here: 66.7 us
  blocking collectives  37.7 us (56%)
  starting transfers between devices  13.3 us (20%)
  Pallas kernels  9.97 us (15%)
  waiting for transfers between devices  5.09 us (8%)
  between operations  0.69 us (1%)
    all_to_all x3, blocking collectives, exchanged(): return lax.all_to_all(blocks, axes, 0, 0, tiled=True).reshape(rows.shape)  37.7 us
    all_to_all x1, starting transfers between devices, shards(): cot = lax.all_to_all(cot, SPACE, 0, 0, tiled=True)  8.67 us
    all_to_all x1, waiting for transfers between devices, shards(): cot = lax.all_to_all(cot, SPACE, 0, 0, tiled=True)  5.08 us
    ppermute x1, starting transfers between devices, passed_along(): return lax.ppermute(block, axis, route)  4.59 us
    pallas_call x1, Pallas kernels, local_message(): call(layers, jax.ShapeDtypeStruct((768, CELLS), BF16), [vmem(*chosen.shap...  4.56 us
    pallas_call x1, Pallas kernels, local_message(): call(prepare, (vmem(15, 9 * ROWS0, CELLS, dtype=BF16), vmem(64, 9 * ROWS0...  2.6 us
    pallas_call x1, Pallas kernels, fetched(): call(fetch, (jax.ShapeDtypeStruct((64, 1, CELLS), F32), vmem(*dens.shape,...  1.73 us
  transfers between devices with their start and end apart: 2, of which 1 were waited for; matrix products, arithmetic and copies ran while one was open for 0% of the time, Pallas kernels for 6%

profile of v2, /device:TPU:1, one launch (start us, length us, event | category | flops | bytes accessed | tf_op | source)
XLA Modules:
  0.0 66.7 jit_solution(12996821821108048453)
XLA Ops:
  0.6 4.6 %collective-permute-start = (bf16[4,8,64,128]{3,2,1,0:T(8,128)(2,1)}, bf16[4,8,64,128]{3,2,1,0:T(8,128)(2,1)S(1)}, u32[]{:S(2)}, u32[]{:S(2)}) collective-permute-start(bf16[4,8,64,128]{3,2,1,0:T(8,128)(2,1)} %bitcast.39), channel_id=1, source_target_pairs={{0,1},{1,2},{2,3},{3,4},{4,5},{5,6},{6,7},{7,8},{8,9},{9,10},{10,1... | collective-permute-start | bytes 1572872 | tf_op jit(solution)/shard_map/ppermute | solution.py:284
  5.2 1.7 %shard_map.93 = (f32[64,1,128]{2,1,0:T(1,128)}, bf16[4,8,64,128]{3,2,1,0:T(8,128)(2,1)S(1)}) custom-call(bf16[128,64]{1,0:T(8,128)(2,1)} %bitcast.43, bf16[4,8,64,128]{3,2,1,0:T(8,128)(2,1)} %bitcast.40), custom_call_target="tpu_custom_call" | custom-call | tf_op jit(solution)/shard_map/pallas_call | solution.py:373
  7.0 8.7 %all-to-all-start = ((f32[64,1,128]{2,1,0:T(1,128)}), f32[64,1,128]{2,1,0:T(1,128)S(1)}, u32[]{:S(2)}, u32[]{:S(2)}) async-start(f32[64,1,128]{2,1,0:T(1,128)} %get-tuple-element.25), calls=%async_computation | async-start | bytes 65536 | tf_op jit(solution)/shard_map/all_to_all | solution.py:443
  15.6 0.0 collective-permute-done.halo_any
  15.7 2.6 %shard_map.94 = (bf16[15,432,128]{2,1,0:T(8,128)(2,1)S(1)}, bf16[64,432]{1,0:T(8,128)(2,1)S(1)}, bf16[720,64]{1,0:T(8,128)(2,1)S(1)}, bf16[864,64]{1,0:T(8,128)(...) custom-call(bf16[4,8,64,128]{3,2,1,0:T(8,128)(2,1)S(1)} %get-tuple-element.18.dens_ref, ...), custom_call_target="tpu_custom_call" | custom-call | tf_op jit(solution)/shard_map/pallas_call | solution.py:388
  18.3 5.1 %all-to-all-done.cot_ref = f32[64,1,128]{2,1,0:T(1,128)S(1)} async-done(((f32[64,1,128]{2,1,0:T(1,128)}), f32[64,1,128]{2,1,0:T(1,128)S(1)}, u32[]{:S(2)}, u32[]{:S(2)}) %all-to-all-start) | async-done | bytes 32800 | tf_op jit(solution)/shard_map/all_to_all | solution.py:443
  23.4 4.6 %shard_map.95 = bf16[768,128]{1,0:T(8,128)(2,1)S(1)} custom-call(bf16[15,432,128]{2,1,0:T(8,128)(2,1)S(1)} %get-tuple-element.19.planes_ref, bf16[64,432]{1,0:T(8,128)(2,1)S(1)} %get-tuple-element.20.w1_ref, bf16[720,64]{1,0:T(8,128)(2,1)S(1)} %get-tuple-element.21.w2_ref, bf16[864,64]{1,0:T(8,128)(2,1)S(1)} %get-tuple-element.22.w3_ref, ...), custom_call_target="tpu_custom_call" | custom-call | tf_op jit(solution)/shard_map/pallas_call | solution.py:409
  27.9 9.8 %all_to_all.20 = bf16[16,48,128]{2,1,0:T(8,128)(2,1)S(1)} all-to-all(bf16[16,48,128]{2,1,0:T(8,128)(2,1)S(1)} %bitcast.34), channel_id=1, replica_groups=mesh['dp'=4,'x'=4,'z'=2,'y'=4,'core'=2] {'z','y','core'}, dimensions={0} | all-to-all | bytes 393216 | tf_op jit(solution)/shard_map/all_to_all | solution.py:434
  37.7 0.1 shard_map.96
  37.8 17.2 %all_to_all.21 = bf16[16,32,128]{2,1,0:T(8,128)(2,1)S(1)} all-to-all(bf16[16,32,128]{2,1,0:T(8,128)(2,1)S(1)} %bitcast.36), channel_id=1, replica_groups=mesh['dp'=4,'x'=4,'z'=2,'y'=4,'core'=2] {'dp','x'}, dimensions={0} | all-to-all | bytes 262144 | tf_op jit(solution)/shard_map/all_to_all | solution.py:434
  55.0 10.7 %all_to_all.22 = f32[16,8,128]{2,1,0:T(8,128)S(1)} all-to-all(f32[16,8,128]{2,1,0:T(8,128)S(1)} %bitcast.38), channel_id=1, replica_groups=mesh['dp'=4,'x'=4,'z'=2,'y'=4,'core'=2] {'z','y','core'}, dimensions={0} | all-to-all | bytes 131072 | tf_op jit(solution)/shard_map/all_to_all | solution.py:434
  65.7 1.0 %shard_map.98 = (bf16[128,64]{1,0:T(8,128)(2,1)}, f32[27,4,16]{2,1,0:T(4,128)}, f32[432,32]{1,0:T(8,128)}, f32[27,1,32]{2,1,0:T(1,128)}) custom-call(s32[1]{0:T(128)} %bitcast.9.dp_ref, bf16[512,128]{1,0:T(8,128)(2,1)S(1)} %bitcast.33, f32[128,128]{1,0:T(8,128)S(1)} %bitcast.37), custom_call_target="tpu_custom_call" | custom-call | tf_op jit(solution)/shard_map/pallas_call | solution.py:451
  (1 shorter events, 0.0 us)
Async XLA Ops:
  0.6 15.0 %collective-permute-start = (bf16[4,8,64,128]{3,2,1,0:T(8,128)(2,1)}, bf16[4,8,64,128]{3,2,1,0:T(8,128)(2,1)S(1)}, u32[]{:S(2)}, u32[]{:S(2)}) collective-permute-start(bf16[4,8,64,128]{3,2,1,0:T(8,128)(2,1)} %bitcast.39), channel_id=1, source_target_pairs={{0,1},{1,2},{2,3},{3,4},{4,5},{5,6},{6,7},{7,8},{8,9},{9,10},{10,1... | collective-permute-start | bytes 1572872 | tf_op jit(solution)/shard_map/ppermute | solution.py:284
  7.0 16.4 %all-to-all-start = ((f32[64,1,128]{2,1,0:T(1,128)}), f32[64,1,128]{2,1,0:T(1,128)S(1)}, u32[]{:S(2)}, u32[]{:S(2)}) async-start(f32[64,1,128]{2,1,0:T(1,128)} %get-tuple-element.25), calls=%async_computation | async-start | bytes 65536 | tf_op jit(solution)/shard_map/all_to_all | solution.py:443

commit v3 on v2

--- a/solution.py
+++ b/solution.py
@@ -261,7 +261,7 @@
             first = got[at : at + 16] if first is None else first + got[at : at + 16]
 
     def put(row, value):
-        whole_ref[pl.ds(row, 16, stride=48), :] = value
+        whole_ref[pl.ds(row, 16, stride=40), :] = value
 
     for x in range(4):
         for r in range(7):
@@ -272,10 +272,8 @@
             value = second[16 * h : 16 * h + 16, 128 * r : 128 * r + 128]
             if r == 3:
                 value = jnp.where(lane_iota(16) < 64, value, pltpu.roll(first, 64, 1) if h == 0 else first)
-            upper = value.astype(BF16).astype(F32)
-            put(32 + 4 * h + r, upper)
-            put(40 + 4 * h + r, value - upper)
-    message_ref[...] = whole_ref[0:768, :].astype(BF16)
+            put(32 + 4 * h + r, value)
+    message_ref[...] = whole_ref[0:640, :].astype(BF16)
 
 
 def passed_along(block, axis, distance):
@@ -294,14 +292,14 @@
 
 
 def regroup(got_ref, message_ref, whole_ref):
-    whole_ref[0:768, :] = got_ref[...].astype(F32)
-    total = whole_ref[0:48, :]
+    whole_ref[0:640, :] = got_ref[...].astype(F32)
+    total = whole_ref[0:40, :]
     for j in range(1, 16):
-        total = total + whole_ref[48 * j : 48 * j + 48, :]
-    shared = total[32:40] + total[40:48]
+        total = total + whole_ref[40 * j : 40 * j + 40, :]
+    shared = total[32:40]
     for x in range(4):
         sums = jnp.concatenate([total[8 * x : 8 * x + 8], shared], axis=0).astype(BF16)
-        feat = whole_ref[pl.ds(8 * x + 7, 16, stride=48), :].astype(BF16)
+        feat = whole_ref[pl.ds(8 * x + 7, 16, stride=40), :].astype(BF16)
         for dp in range(4):
             base = 128 * dp + 32 * x
             message_ref[base : base + 16, :] = sums
@@ -408,7 +406,7 @@
     )(in_vmem(dens), halo, *map(in_hbm, arguments[1:]))
     return call(
         layers,
-        jax.ShapeDtypeStruct((768, CELLS), BF16),
+        jax.ShapeDtypeStruct((640, CELLS), BF16),
         [
             vmem(*chosen.shape, dtype=BF16),
             pltpu.SemaphoreType.DMA,
@@ -421,7 +419,7 @@
             vmem(9 * ROWS2, CELLS),
             vmem(9 * ROWS1, 768),
             vmem(64, 3584, dtype=BF16),
-            vmem(816, CELLS),
+            vmem(688, CELLS),
         ],
         26,
         in_specs=[IN_VMEM] * 7 + [IN_HBM],
@@ -444,7 +442,7 @@
     message = local_message(halo, dens, first_kernel, second_kernel, third_kernel, cot)
     message, dp = lax.optimization_barrier((message, lax.axis_index("dp").reshape(1)))
     got = exchanged(message, NEAR)
-    got = exchanged(call(regroup, shape((512, CELLS), BF16), [vmem(816, CELLS)])(got), FAR)
+    got = exchanged(call(regroup, shape((512, CELLS), BF16), [vmem(688, CELLS)])(got), FAR)
     both = exchanged(call(share, shape((CELLS, CELLS), F32))(got), NEAR)
     outs = (shape((CELLS, 64), BF16), shape((27, 4, 16), F32), shape((432, 32), F32), shape((27, 1, 32), F32))
     specs = [pl.BlockSpec(memory_space=pltpu.SMEM), pl.BlockSpec(), pl.BlockSpec()]

time: 67 us -> 66.6 us (level)
  transfers between devices with their start and end apart: 2 -> 2, of which waited for: 1 -> 1; matrix products, arithmetic and copies ran while one was open for 0% -> 0% of each run, Pallas kernels for 6% -> 7%
where the time goes in v3:
time: 66.6 us; the launch traced here: 66.3 us
  blocking collectives  37.3 us (56%)
  starting transfers between devices  13.3 us (20%)
  Pallas kernels  9.9 us (15%)
  waiting for transfers between devices  5.09 us (8%)
  between operations  0.69 us (1%)
    all_to_all x3, blocking collectives, exchanged(): return lax.all_to_all(blocks, axes, 0, 0, tiled=True).reshape(rows.shape)  37.3 us
    all_to_all x1, starting transfers between devices, shards(): cot = lax.all_to_all(cot, SPACE, 0, 0, tiled=True)  8.67 us
    all_to_all x1, waiting for transfers between devices, shards(): cot = lax.all_to_all(cot, SPACE, 0, 0, tiled=True)  5.08 us
    ppermute x1, starting transfers between devices, passed_along(): return lax.ppermute(block, axis, route)  4.59 us
    pallas_call x1, Pallas kernels, local_message(): call(layers, jax.ShapeDtypeStruct((640, CELLS), BF16), [vmem(*chosen.shap...  4.5 us
    pallas_call x1, Pallas kernels, local_message(): call(prepare, (vmem(15, 9 * ROWS0, CELLS, dtype=BF16), vmem(64, 9 * ROWS0...  2.6 us
    pallas_call x1, Pallas kernels, fetched(): call(fetch, (jax.ShapeDtypeStruct((64, 1, CELLS), F32), vmem(*dens.shape,...  1.73 us
  transfers between devices with their start and end apart: 2, of which 1 were waited for; matrix products, arithmetic and copies ran while one was open for 0% of the time, Pallas kernels for 7%

profile of v3, /device:TPU:1, one launch (start us, length us, event | category | flops | bytes accessed | tf_op | source)
XLA Modules:
  0.0 66.3 jit_solution(2170822010479974753)
XLA Ops:
  0.6 4.6 %collective-permute-start = (bf16[4,8,64,128]{3,2,1,0:T(8,128)(2,1)}, bf16[4,8,64,128]{3,2,1,0:T(8,128)(2,1)S(1)}, u32[]{:S(2)}, u32[]{:S(2)}) collective-permute-start(bf16[4,8,64,128]{3,2,1,0:T(8,128)(2,1)} %bitcast.39), channel_id=1, source_target_pairs={{0,1},{1,2},{2,3},{3,4},{4,5},{5,6},{6,7},{7,8},{8,9},{9,10},{10,1... | collective-permute-start | bytes 1572872 | tf_op jit(solution)/shard_map/ppermute | solution.py:282
  5.2 1.7 %shard_map.93 = (f32[64,1,128]{2,1,0:T(1,128)}, bf16[4,8,64,128]{3,2,1,0:T(8,128)(2,1)S(1)}) custom-call(bf16[128,64]{1,0:T(8,128)(2,1)} %bitcast.43, bf16[4,8,64,128]{3,2,1,0:T(8,128)(2,1)} %bitcast.40), custom_call_target="tpu_custom_call" | custom-call | tf_op jit(solution)/shard_map/pallas_call | solution.py:371
  7.0 8.7 %all-to-all-start = ((f32[64,1,128]{2,1,0:T(1,128)}), f32[64,1,128]{2,1,0:T(1,128)S(1)}, u32[]{:S(2)}, u32[]{:S(2)}) async-start(f32[64,1,128]{2,1,0:T(1,128)} %get-tuple-element.25), calls=%async_computation | async-start | bytes 65536 | tf_op jit(solution)/shard_map/all_to_all | solution.py:441
  15.6 0.0 collective-permute-done.halo_any
  15.7 2.6 %shard_map.94 = (bf16[15,432,128]{2,1,0:T(8,128)(2,1)S(1)}, bf16[64,432]{1,0:T(8,128)(2,1)S(1)}, bf16[720,64]{1,0:T(8,128)(2,1)S(1)}, bf16[864,64]{1,0:T(8,128)(...) custom-call(bf16[4,8,64,128]{3,2,1,0:T(8,128)(2,1)S(1)} %get-tuple-element.18.dens_ref, ...), custom_call_target="tpu_custom_call" | custom-call | tf_op jit(solution)/shard_map/pallas_call | solution.py:386
  18.3 5.1 %all-to-all-done.cot_ref = f32[64,1,128]{2,1,0:T(1,128)S(1)} async-done(((f32[64,1,128]{2,1,0:T(1,128)}), f32[64,1,128]{2,1,0:T(1,128)S(1)}, u32[]{:S(2)}, u32[]{:S(2)}) %all-to-all-start) | async-done | bytes 32800 | tf_op jit(solution)/shard_map/all_to_all | solution.py:441
  23.4 4.5 %shard_map.95 = bf16[640,128]{1,0:T(8,128)(2,1)S(1)} custom-call(bf16[15,432,128]{2,1,0:T(8,128)(2,1)S(1)} %get-tuple-element.19.planes_ref, bf16[64,432]{1,0:T(8,128)(2,1)S(1)} %get-tuple-element.20.w1_ref, bf16[720,64]{1,0:T(8,128)(2,1)S(1)} %get-tuple-element.21.w2_ref, bf16[864,64]{1,0:T(8,128)(2,1)S(1)} %get-tuple-element.22.w3_ref, ...), custom_call_target="tpu_custom_call" | custom-call | tf_op jit(solution)/shard_map/pallas_call | solution.py:407
  27.9 9.6 %all_to_all.20 = bf16[16,40,128]{2,1,0:T(8,128)(2,1)S(1)} all-to-all(bf16[16,40,128]{2,1,0:T(8,128)(2,1)S(1)} %bitcast.34), channel_id=1, replica_groups=mesh['dp'=4,'x'=4,'z'=2,'y'=4,'core'=2] {'z','y','core'}, dimensions={0} | all-to-all | bytes 327680 | tf_op jit(solution)/shard_map/all_to_all | solution.py:432
  37.5 17.2 %all_to_all.21 = bf16[16,32,128]{2,1,0:T(8,128)(2,1)S(1)} all-to-all(bf16[16,32,128]{2,1,0:T(8,128)(2,1)S(1)} %bitcast.36), channel_id=1, replica_groups=mesh['dp'=4,'x'=4,'z'=2,'y'=4,'core'=2] {'dp','x'}, dimensions={0} | all-to-all | bytes 262144 | tf_op jit(solution)/shard_map/all_to_all | solution.py:432
  54.7 10.6 %all_to_all.22 = f32[16,8,128]{2,1,0:T(8,128)S(1)} all-to-all(f32[16,8,128]{2,1,0:T(8,128)S(1)} %bitcast.38), channel_id=1, replica_groups=mesh['dp'=4,'x'=4,'z'=2,'y'=4,'core'=2] {'z','y','core'}, dimensions={0} | all-to-all | bytes 131072 | tf_op jit(solution)/shard_map/all_to_all | solution.py:432
  65.3 1.0 %shard_map.98 = (bf16[128,64]{1,0:T(8,128)(2,1)}, f32[27,4,16]{2,1,0:T(4,128)}, f32[432,32]{1,0:T(8,128)}, f32[27,1,32]{2,1,0:T(1,128)}) custom-call(s32[1]{0:T(128)} %bitcast.9.dp_ref, bf16[512,128]{1,0:T(8,128)(2,1)S(1)} %bitcast.33, f32[128,128]{1,0:T(8,128)S(1)} %bitcast.37), custom_call_target="tpu_custom_call" | custom-call | tf_op jit(solution)/shard_map/pallas_call | solution.py:449
  (2 shorter events, 0.1 us)
Async XLA Ops:
  0.6 15.0 %collective-permute-start = (bf16[4,8,64,128]{3,2,1,0:T(8,128)(2,1)}, bf16[4,8,64,128]{3,2,1,0:T(8,128)(2,1)S(1)}, u32[]{:S(2)}, u32[]{:S(2)}) collective-permute-start(bf16[4,8,64,128]{3,2,1,0:T(8,128)(2,1)} %bitcast.39), channel_id=1, source_target_pairs={{0,1},{1,2},{2,3},{3,4},{4,5},{5,6},{6,7},{7,8},{8,9},{9,10},{10,1... | collective-permute-start | bytes 1572872 | tf_op jit(solution)/shard_map/ppermute | solution.py:282
  7.0 16.4 %all-to-all-start = ((f32[64,1,128]{2,1,0:T(1,128)}), f32[64,1,128]{2,1,0:T(1,128)S(1)}, u32[]{:S(2)}, u32[]{:S(2)}) async-start(f32[64,1,128]{2,1,0:T(1,128)} %get-tuple-element.25), calls=%async_computation | async-start | bytes 65536 | tf_op jit(solution)/shard_map/all_to_all | solution.py:441
